TPU v7x, 512 devices: a whole 4x8x8 slice. The times are simulated.
512 devices in a mesh: context: 64 (over z, y_hi, core), tensor: 8 (over y_lo, x).
Axes of the slice: x: 4, y: 8 (y_hi: 4, y_lo: 2; y = y_hi * 2 + y_lo), z: 8, core: 2. Of those that a mesh axis runs over, the one named last changes fastest.
Arguments:
- hidden_rows: bfloat16 [8192, 4096], P(('context', 'tensor')), may hold values from -6 to 6
- norm_gain: bfloat16 [4096], replicated, may hold values from 0.25 to 1.75
- w_qkv: bfloat16 [4096, 6144], P('context', 'tensor')
- w_out: bfloat16 [4096, 4096], P('tensor', 'context'), may hold values from -0.09375 to 0.09375
- doc_lengths: int32 [16], replicated, may hold values from 1 to 2048, 8192 in all
- span_order: int32 [128], replicated, may hold values from 0 to 127, each once
Outputs:
- attended: bfloat16 [8192, 4096], P(('context', 'tensor'))
Inputs may be any that keep to these rules, and one draw needn't show every extreme that they name: `doc_lengths`: the lengths sum to 8192; the longest is exactly 2048. `span_order`: each initial span appears once.
All inputs are finite; a program needn't handle non-finite values.
Results may differ from a plain program's by a relative error of at most 0.02.
The roundings to bfloat16 on the way count: a program that leaves them out, or rounds other values in their place, can miss the bound.
Values may be sent and summed in bfloat16 or wider, within the bound.
A program may use at most 64 MiB of HBM per device.

v0:
```python
import jax
import jax.numpy as jnp
from jax import lax
from jax.sharding import PartitionSpec as P

HD = 128
QH_DEV = 4
SPAN = 64


rope_theta = 500000.0


def locate(layout_rows, span_order, doc_ends):
    span_index = layout_rows // SPAN
    matches = span_index[:, None] == jnp.arange(span_order.shape[0], dtype=jnp.int32)[None, :]
    source_span = jnp.sum(jnp.where(matches, span_order[None, :], 0), axis=1)
    initial = source_span * SPAN + layout_rows % SPAN
    document = jnp.sum((initial[:, None] >= doc_ends[None, :]).astype(jnp.int32), axis=1)
    doc_start = jnp.max(
        jnp.where(doc_ends[None, :] <= initial[:, None], doc_ends[None, :], 0), axis=1
    )
    return (initial, document, initial - doc_start)


def rotate(values, position):
    half = values.shape[-1] // 2
    freq = rope_theta ** (-(jnp.arange(half, dtype=jnp.float32) * 2.0 / values.shape[-1]))
    angle = position.astype(jnp.float32)[:, None, None] * freq[None, None, :]
    cosine = jnp.cos(angle)
    sine = jnp.sin(angle)
    first_half = values[..., :half]
    second_half = values[..., half:]
    return jnp.concatenate(
        [first_half * cosine - second_half * sine, second_half * cosine + first_half * sine],
        axis=-1,
    )


def per_device(hidden_rows, norm_gain, w_qkv, w_out, doc_lengths, span_order):
    doc_ends = jnp.cumsum(doc_lengths)
    wide = hidden_rows.astype(jnp.float32)
    meansq = jnp.mean(wide * wide, axis=-1, keepdims=True)
    normed = (wide * lax.rsqrt(meansq + 1e-05) * norm_gain.astype(jnp.float32)[None, :]).astype(
        jnp.bfloat16
    )
    normed_all = lax.all_gather(normed, "tensor", axis=0, tiled=True)
    tokens_here = normed_all.shape[0]
    head_cols = QH_DEV * HD
    qkv = jnp.dot(
        normed_all,
        lax.all_gather(w_qkv, "context", axis=0, tiled=True),
        preferred_element_type=jnp.float32,
    )
    first_layout = lax.axis_index("context") * tokens_here
    query_rows = first_layout + jnp.arange(tokens_here, dtype=jnp.int32)
    query_orig, query_doc, query_pos = locate(query_rows, span_order, doc_ends)
    queries = rotate(qkv[:, :head_cols].reshape(tokens_here, QH_DEV, HD), query_pos).astype(
        jnp.bfloat16
    )
    keys = rotate(qkv[:, head_cols : head_cols + HD].reshape(tokens_here, 1, HD), query_pos)
    keys = keys.reshape(tokens_here, HD).astype(jnp.bfloat16)
    values = qkv[:, head_cols + HD :].astype(jnp.bfloat16)
    scale = 1.0 / HD**0.5
    key_block = lax.all_gather(keys, "context", axis=0, tiled=True)
    value_block = lax.all_gather(values, "context", axis=0, tiled=True)
    count = key_block.shape[0]
    key_rows = jnp.arange(count, dtype=jnp.int32)
    key_orig, key_doc, unused_pos = locate(key_rows, span_order, doc_ends)
    allowed = (key_doc[None, :] == query_doc[:, None]) & (key_orig[None, :] <= query_orig[:, None])
    top_old = jnp.full((tokens_here, QH_DEV), -1e30, jnp.float32)
    scores = (
        jnp.einsum("qhd,kd->qhk", queries, key_block, preferred_element_type=jnp.float32) * scale
    )
    scores = jnp.where(allowed[:, None, :], scores, -1e30)
    top_new = jnp.maximum(top_old, jnp.max(scores, axis=-1))
    expo = jnp.where(allowed[:, None, :], jnp.exp(scores - top_new[..., None]), 0.0)
    total_new = jnp.sum(expo, axis=-1)
    product = jnp.einsum(
        "qhk,kd->qhd", expo.astype(jnp.bfloat16), value_block, preferred_element_type=jnp.float32
    )
    mixed = (product / total_new[..., None]).astype(jnp.bfloat16).reshape(tokens_here, head_cols)
    partial_sums = jnp.dot(
        mixed,
        lax.all_gather(w_out, "context", axis=1, tiled=True),
        preferred_element_type=jnp.float32,
    )
    return lax.psum_scatter(
        partial_sums.astype(jnp.bfloat16), "tensor", scatter_dimension=0, tiled=True
    )


def solution(mesh):
    placed = (
        P(("context", "tensor"), None),
        P(),
        P("context", "tensor"),
        P("tensor", "context"),
        P(),
        P(),
    )
    return jax.shard_map(
        per_device,
        mesh=mesh,
        in_specs=placed,
        out_specs=P(("context", "tensor"), None),
        check_vma=False,
    )
```

profile of v0, /device:TPU:1, one launch (start us, length us, event | category | flops | bytes accessed | tf_op | source)
XLA Modules:
  0.0 457.3 jit_solution(17642520207154829159)
XLA Ops:
  6.5 0.0 copy-start.1
  6.5 0.0 all-gather.7.cloned.1.call-start
  6.5 0.7 convert_element_type.41
  7.2 1.0 fusion.19
  8.3 1.7 fusion.21
  10.0 0.0 all-gather.7.cloned.1.call-update
  10.0 0.0 all-gather.9.cloned.1.call-start
  10.0 0.7 all-gather.9.cloned.1.call-update
  10.7 0.0 all-gather.15.cloned.1.call-start
  10.8 0.7 copy.19
  11.6 0.1 reduce
  11.7 0.8 select_reduce_fusion.1
  12.6 0.1 convert_reduce_fusion.1
  12.7 42.1 %all-gather.7.cloned.1.call-done = bf16[128,4096]{1,0:T(8,128)(2,1)} async-done(((bf16[16,4096]{1,0:T(8,128)(2,1)}), bf16[128,4096]{1,0:T(8,128)(2,1)}) %all-gather.7.cloned.1.call-update) | async-done | bytes 1048592 | tf_op jit(solution)/shard_map/all_gather | solution.py:47
  54.8 102.9 %all-gather.9.cloned.1.call-done = bf16[4096,768]{1,0:T(8,128)(2,1)} async-done(((bf16[64,768]{1,0:T(8,128)(2,1)}), bf16[4096,768]{1,0:T(8,128)(2,1)}) %all-gather.9.cloned.1.call-update) | async-done | bytes 6291472 | tf_op jit(solution)/shard_map/all_gather | solution.py:52
  157.7 4.1 fusion.47
  161.9 0.1 copy.31
  162.0 0.2 fusion.36
  162.2 0.6 pad_maximum_fusion
  162.8 0.0 all-gather.15.cloned.1.call-update
  162.8 0.0 all-gather.11.cloned.1.call-start
  162.9 0.6 slice.41
  163.5 0.0 all-gather.11.cloned.1.call-update
  163.5 0.0 all-gather.13.cloned.1.call-start
  163.6 0.5 all-gather.13.cloned.1.call-update
  164.1 0.0 reduce-scatter.2.cloned.1.call-start
  164.2 0.0 copy-done.1
  164.2 2.5 select_reduce_fusion
  166.7 0.2 convert_reduce_fusion
  166.9 0.3 multiply_cosine_fusion
  167.2 0.9 compare_and_fusion
  168.1 0.1 reshape.306
  168.2 0.2 fusion.46
  168.4 0.1 subtract_convert_fusion
  168.5 70.3 %all-gather.15.cloned.1.call-done = bf16[8192,1,128]{0,2,1:T(8,128)(2,1)} async-done(((bf16[128,1,128]{0,2,1:T(8,128)(2,1)}), bf16[8192,1,128]{0,2,1:T(8,128)(2,1)}) %all-gather.15.cloned.1.call-update) | async-done | bytes 2097168 | tf_op jit(solution)/shard_map/all_gather | solution.py:65
  238.8 5.0 %fusion = (f32[128,4]{0,1:T(4,128)S(1)}, f32[128,4,8192]{2,0,1:T(8,128)S(1)}) fusion(pred[128,8192]{1,0:T(8,128)(4,1)S(1)} %compare_and_fusion, bf16[8192,1,128]{0,2,1:T(8,128)(2,1)} %all-gather.15.cloned.1.call-done, bf16[128,4,64]{2,0,1:T(8,128)(2,1)S(1)} %get-tuple-element.8, bf16[128,4,64]{2,0,1:T(8,128)(2,1)S(1)} %get-tuple-element.7), kind=kOutput, calls=%fused_computation.2 | convolution fusion | flops 1086586368 | bytes 20056064 | tf_op jit(solution)/shard_map/qhd,kd->qhk/dot_general | solution.py:73
  243.8 0.0 copy-start
  243.8 5.7 %copy-done = f32[128,4,8192]{2,0,1:T(8,128)} copy-done((f32[128,4,8192]{2,0,1:T(8,128)}, f32[128,4,8192]{2,0,1:T(8,128)S(1)}, u32[]{:S(2)}) %copy-start) | copy-done | bytes 16777240
  249.5 5.1 %fusion.1 = f32[128,4]{0,1:T(4,128)S(1)} fusion(f32[128,4,8192]{2,0,1:T(8,128)S(1)} %get-tuple-element.16, f32[128,4]{0,1:T(4,128)S(1)} %broadcast_maximum_fusion, pred[128,8192]{1,0:T(8,128)(4,1)S(1)} %compare_and_fusion), kind=kLoop, calls=%fused_computation.3 | loop fusion | flops 20971008 | bytes 17829888 | tf_op jit(solution)/shard_map/reduce_sum | solution.py:78
  254.6 69.2 %all-gather.11.cloned.1.call-done = bf16[8192,128]{1,0:T(8,128)(2,1)} async-done(((bf16[128,128]{1,0:T(8,128)(2,1)}), bf16[8192,128]{1,0:T(8,128)(2,1)}) %all-gather.11.cloned.1.call-update) | async-done | bytes 2097168 | tf_op jit(solution)/shard_map/all_gather | solution.py:66
  323.8 10.0 %fusion.14 = bf16[128,4,128]{0,2,1:T(8,128)(2,1)S(1)} fusion(bf16[8192,128]{1,0:T(8,128)(2,1)} %all-gather.11.cloned.1.call-done, f32[128,4,8192]{2,0,1:T(8,128)} %copy-done, f32[128,4]{0,1:T(4,128)S(1)} %broadcast_maximum_fusion, pred[128,8192]{1,0:T(8,128)(4,1)S(1)} %compare_and_fusion, f32[128,4]{0,1:T(4,128)S(1)} %fusion.1), kind=kOutput, calls=%fused_computation.15 | convolution fusion | flops 1094844416 | bytes 20058112 | tf_op jit(solution)/shard_map/qhk,kd->qhd/dot_general | solution.py:79
  333.8 76.4 %all-gather.13.cloned.1.call-done = bf16[512,4096]{0,1:T(8,128)(2,1)} async-done(((bf16[512,64]{0,1:T(8,128)(2,1)}), bf16[512,4096]{0,1:T(8,128)(2,1)}) %all-gather.13.cloned.1.call-update) | async-done | bytes 4194320 | tf_op jit(solution)/shard_map/all_gather | solution.py:85
  410.1 4.7 %convolution_convert_fusion = bf16[128,4096]{1,0:T(8,128)(2,1)} fusion(bf16[128,512]{0,1:T(8,128)(2,1)S(1)} %bitcast.22, bf16[512,4096]{0,1:T(8,128)(2,1)} %all-gather.13.cloned.1.call-done), kind=kOutput, calls=%fused_computation.7 | convolution fusion | flops 537395200 | bytes 5373952 | tf_op jit(solution)/shard_map/dot_general | solution.py:83
  414.9 0.0 reduce-scatter.2.cloned.1.call-update
  414.9 35.6 %reduce-scatter.2.cloned.1.call-done = bf16[16,4096]{1,0:T(8,128)(2,1)} async-done(((bf16[128,4096]{1,0:T(8,128)(2,1)}), bf16[16,4096]{1,0:T(8,128)(2,1)}) %reduce-scatter.2.cloned.1.call-update) | async-done | bytes 131088 | tf_op jit(solution)/shard_map/reduce_scatter | solution.py:88
  (11 shorter events, 0.1 us)
Async XLA Ops:
  6.5 157.6 %copy-start.1 = (s32[128]{0:T(128)S(1)}, s32[128]{0:T(128)}, u32[]{:S(2)}) copy-start(s32[128]{0:T(128)} %param.11) | copy-start | bytes 1540
  6.5 48.3 %all-gather.7.cloned.1.call-start = ((), (), s32[]{:S(2)}) async-start(), calls=%async_computation.1 | async-start | bytes 1179648 | tf_op jit(solution)/shard_map/all_gather | solution.py:47
  10.0 147.8 %all-gather.9.cloned.1.call-start = ((), (), s32[]{:S(2)}) async-start(), calls=%async_computation.2 | async-start | bytes 6389760 | tf_op jit(solution)/shard_map/all_gather | solution.py:52
  10.7 228.1 %all-gather.15.cloned.1.call-start = ((), (), s32[]{:S(2)}) async-start(), calls=%async_computation.6 | async-start | bytes 2129920 | tf_op jit(solution)/shard_map/all_gather | solution.py:65
  162.8 161.0 %all-gather.11.cloned.1.call-start = ((), (), s32[]{:S(2)}) async-start(), calls=%async_computation.3 | async-start | bytes 2129920 | tf_op jit(solution)/shard_map/all_gather | solution.py:66
  163.5 246.6 %all-gather.13.cloned.1.call-start = ((), (), s32[]{:S(2)}) async-start(), calls=%async_computation.4 | async-start | bytes 4259840 | tf_op jit(solution)/shard_map/all_gather | solution.py:85
  164.1 286.4 %reduce-scatter.2.cloned.1.call-start = ((), (), s32[]{:S(2)}) async-start(), calls=%async_computation.5 | async-start | bytes 1179648 | tf_op jit(solution)/shard_map/reduce_scatter | solution.py:88
  243.8 5.7 %copy-start = (f32[128,4,8192]{2,0,1:T(8,128)}, f32[128,4,8192]{2,0,1:T(8,128)S(1)}, u32[]{:S(2)}) copy-start(f32[128,4,8192]{2,0,1:T(8,128)S(1)} %get-tuple-element.16) | copy-start | bytes 50331652
Sparse Core Ops, SparseCore 0:
  10.1 44.6 all-gather.6
  58.1 99.5 all-gather.8
  162.9 75.8 all-gather.14
  242.0 81.7 all-gather.10
  327.0 83.1 all-gather.12
  415.0 35.4 reduce-scatter.1
where the time goes:
time: 461 us; the launch traced here: 457 us
  waiting for transfers between devices  398 us (86%)
  matrix products  23.8 us (5%)
  other arithmetic  14.4 us (3%)
  between operations  13.6 us (3%)
  local copies, waits for them, and re-layouts  7.46 us (2%)
    all_gather x1, waiting for transfers between devices, per_device(): lax.all_gather(w_qkv, 'context', axis=0, tiled=True)  103 us
    all_gather x1, waiting for transfers between devices, per_device(): lax.all_gather(w_out, 'context', axis=1, tiled=True)  76.4 us
    all_gather x1, waiting for transfers between devices, per_device(): key_block = lax.all_gather(keys, 'context', axis=0, tiled=True)  70.3 us
    all_gather x1, waiting for transfers between devices, per_device(): value_block = lax.all_gather(values, 'context', axis=0, tiled=True)  69.2 us
    all_gather x1, waiting for transfers between devices, per_device(): normed_all = lax.all_gather(normed, 'tensor', axis=0, tiled=True)  42.1 us
    reduce_scatter x1, waiting for transfers between devices, per_device(): lax.psum_scatter(partial_sums.astype(jnp.bfloat16), 'tensor', scatter_dim...  35.6 us
    dot_general x1, matrix products, per_device(): jnp.einsum('qhk,kd->qhd', expo.astype(jnp.bfloat16), value_block, preferr...  9.98 us
  transfers between devices with their start and end apart: 6, of which 6 were waited for; matrix products, arithmetic and copies ran while one was open for 6% of the time, Pallas kernels for 0%

commit v1 on v0

v1 whole, which is shorter than its diff:
```python
import functools
import math

import jax
import jax.numpy as jnp
import numpy as np
from jax import lax
from jax.experimental import pallas as pl
from jax.experimental.pallas import tpu as pltpu
from jax.sharding import PartitionSpec as P

HD = 128
HEADS_HERE = 4
SPAN = 64
THETA = 500000.0
Y_HI = 4
CORES = 2
MASKED = -1e30
NT_DIMS = (((1,), (1,)), ((), ()))

W_IN, KV, W_OUT = 0, 1, 2


def kernel(
    NZ,
    NY,
    NT,
    span_ref,
    len_ref,
    hidden_ref,
    gain_ref,
    freq_ref,
    w_in_ref,
    w_out_ref,
    out_ref,
    w_in_own,
    w_in_sib,
    kv_own,
    kv_sib,
    w_out_own,
    w_out_sib,
    normed_ref,
    acc_ref,
    q_ref,
    kv_stage,
    o_ref,
    top_ref,
    sum_ref,
    mixed_ref,
    rs_send,
    rs_recv,
    own_recv,
    sib_recv,
    plane_send,
    ring_send,
    sib_send,
    norm_send,
    norm_recv,
    rs_send_sem,
    rs_recv_sem,
):
    PLANE = NY * CORES
    J = PLANE // 2
    rows, D = hidden_ref.shape
    tokens = rows * NT
    qcols = HEADS_HERE * HD
    half_k = J * w_in_ref.shape[0]
    half_c = J * w_out_ref.shape[0]

    ctx = lax.axis_index("context")
    t = lax.axis_index("tensor")
    z = ctx // PLANE
    y = (ctx % PLANE) // CORES
    core = ctx % CORES
    my_class = y // (NY // 2)
    slot = (y % (NY // 2)) * CORES + core
    step_z = 1 - 2 * core
    ahead = ((z + step_z + NZ) % NZ) * PLANE + y * CORES + core
    behind = ((z - step_z + NZ) % NZ) * PLANE + y * CORES + core
    sibling = z * PLANE + y * CORES + (1 - core)

    def device(c, u):
        return {"context": c, "tensor": u}

    own = (w_in_own, kv_own, w_out_own)
    sib = (w_in_sib, kv_sib, w_out_sib)

    barrier = pltpu.get_barrier_semaphore()
    for d in range(1, PLANE):
        c = z * PLANE + (ctx % PLANE + d) % PLANE
        pl.semaphore_signal(barrier, inc=1, device_id=device(c, t))
    for c in (ahead, behind):
        pl.semaphore_signal(barrier, inc=1, device_id=device(c, t))
    for d in range(1, NT):
        pl.semaphore_signal(barrier, inc=1, device_id=device(ctx, (t + d) % NT))

    wide = hidden_ref[...].astype(jnp.float32)
    meansq = jnp.mean(wide * wide, axis=-1, keepdims=True)
    normed = wide * lax.rsqrt(meansq + 1e-5) * gain_ref[...].astype(jnp.float32).reshape(1, D)
    normed_ref[t] = normed.astype(jnp.bfloat16)

    pl.semaphore_wait(barrier, PLANE - 1 + 2 + NT - 1)

    def plane_copy(g, src, d):
        c = z * PLANE + ((y + d) % NY) * CORES + my_class
        return pltpu.make_async_remote_copy(
            src_ref=src,
            dst_ref=own[g].at[0, slot],
            send_sem=plane_send.at[g, d],
            recv_sem=own_recv.at[g, 0, slot],
            device_id=device(c, t),
        )

    def plane_local(g, src):
        return pltpu.make_async_copy(src, own[g].at[0, slot], own_recv.at[g, 0, slot])

    def start_plane(g, src):
        @pl.when(core == my_class)
        def _():
            plane_local(g, src).start()

        @pl.when(core != my_class)
        def _():
            plane_copy(g, src, 0).start()

        for d in range(1, NY):
            plane_copy(g, src, d).start()

    def finish_plane(g, src):
        @pl.when(core != my_class)
        def _():
            plane_copy(g, src, 0).wait_send()

        for d in range(1, NY):
            plane_copy(g, src, d).wait_send()

    def pass_on(g, s):
        for j in range(J):
            unit = own[g].at[s, j]
            pltpu.make_async_copy(unit, unit, own_recv.at[g, s, j]).wait()

            @pl.when(s < NZ - 1)
            def _():
                pltpu.make_async_remote_copy(
                    src_ref=unit,
                    dst_ref=own[g].at[s + 1, j],
                    send_sem=ring_send.at[g],
                    recv_sem=own_recv.at[g, s + 1, j],
                    device_id=device(ahead, t),
                ).start()

            pltpu.make_async_remote_copy(
                src_ref=unit,
                dst_ref=sib[g].at[s, j],
                send_sem=sib_send.at[g],
                recv_sem=sib_recv.at[g, s],
                device_id=device(sibling, t),
            ).start()

    def wait_sibling(g, s):
        whole = sib[g].at[s]
        pltpu.make_async_copy(whole, whole, sib_recv.at[g, s]).wait()

    def finish_gather(g):
        sent = own[g].at[pl.ds(0, NZ - 1)]
        pltpu.make_async_copy(sent, sent, ring_send.at[g]).wait()
        pltpu.make_async_copy(sib[g], sib[g], sib_send.at[g]).wait()

    def own_half(s):
        return ((z - step_z * s + NZ) % NZ) * 2 + core

    def sib_half(s):
        return ((z + step_z * s + NZ) % NZ) * 2 + 1 - core

    start_plane(W_IN, w_in_ref)

    def norm_copy(d):
        return pltpu.make_async_remote_copy(
            src_ref=normed_ref.at[t],
            dst_ref=normed_ref.at[t],
            send_sem=norm_send.at[d - 1],
            recv_sem=norm_recv.at[t],
            device_id=device(ctx, (t + d) % NT),
        )

    for d in range(1, NT):
        norm_copy(d).start()

    start_plane(W_OUT, w_out_ref)

    acc_ref[...] = jnp.zeros_like(acc_ref)
    for d in range(1, NT):
        block = normed_ref.at[(t + NT - d) % NT]
        pltpu.make_async_copy(block, block, norm_recv.at[(t + NT - d) % NT]).wait()

    def project(s):
        wait_sibling(W_IN, s)
        total = acc_ref[...]
        for half, ref in ((own_half(s), w_in_own), (sib_half(s), w_in_sib)):
            cols = pl.ds(pl.multiple_of(half * half_k, half_k), half_k)
            left = normed_ref[:, :, cols].reshape(tokens, half_k)
            right = ref[s].reshape(half_k, ref.shape[-1])
            total += jnp.dot(left, right, preferred_element_type=jnp.float32)
        acc_ref[...] = total

    def project_step(s, carry):
        pass_on(W_IN, s)

        @pl.when(s > 0)
        def _():
            project(s - 1)

        return carry

    lax.fori_loop(0, NZ, project_step, 0)
    pass_on(W_OUT, 0)
    project(NZ - 1)

    row = lax.broadcasted_iota(jnp.int32, (tokens, 1), 0)
    source = jnp.zeros_like(row)
    for a in range(tokens // SPAN):
        source = jnp.where(row // SPAN == a, span_ref[ctx * (tokens // SPAN) + a], source)
    orig = source * SPAN + row % SPAN
    start = jnp.zeros_like(orig)
    end = jnp.int32(0)
    for i in range(len_ref.shape[0]):
        end = end + len_ref[i]
        start = jnp.where(end <= orig, jnp.maximum(start, end), start)

    angle = (orig - start).astype(jnp.float32) * freq_ref[...]
    lane = lax.broadcasted_iota(jnp.int32, (tokens, HD), 1)
    cosine = jnp.cos(angle)
    sine = jnp.where(lane < HD // 2, -jnp.sin(angle), jnp.sin(angle))

    def rotate(x):
        return (x * cosine + pltpu.roll(x, HD // 2, 1) * sine).astype(jnp.bfloat16)

    kv_stage[:, :HD] = rotate(acc_ref[:, qcols : qcols + HD])
    kv_stage[:, HD:] = acc_ref[:, qcols + HD :].astype(jnp.bfloat16)
    start_plane(KV, kv_stage)
    for h in range(HEADS_HERE):
        q_ref[h * tokens : (h + 1) * tokens, :] = rotate(acc_ref[:, h * HD : (h + 1) * HD])

    top_ref[...] = jnp.full_like(top_ref, MASKED)
    sum_ref[...] = jnp.zeros_like(sum_ref)
    o_ref[...] = jnp.zeros_like(o_ref)
    keys = J * tokens
    scale = math.log2(math.e) / HD**0.5

    def attend_half(half, ref, s):
        lane = lax.broadcasted_iota(jnp.int32, (1, keys), 1)
        key_source = jnp.zeros_like(lane)
        spans = keys // SPAN
        for a in range(spans):
            key_source = jnp.where(lane // SPAN == a, span_ref[half * spans + a], key_source)
        key_orig = key_source * SPAN + lane % SPAN
        allowed = (start <= key_orig) & (key_orig <= orig)
        k = ref[s, :, :, :HD].reshape(keys, HD)
        v = ref[s, :, :, HD:].reshape(keys, HD)
        for h in range(HEADS_HERE):
            at = pl.ds(h * tokens, tokens)
            scores = lax.dot_general(q_ref[at, :], k, NT_DIMS, preferred_element_type=jnp.float32)
            scores = jnp.where(allowed, scores, MASKED)
            old = top_ref[at, :]
            new = jnp.maximum(old, jnp.max(scores, axis=1, keepdims=True))
            expo = jnp.exp2((scores - new) * scale)
            fade = jnp.exp2((old - new) * scale)
            top_ref[at, :] = new
            sum_ref[at, :] = sum_ref[at, :] * fade + jnp.sum(expo, axis=1, keepdims=True)
            o_ref[at, :] = o_ref[at, :] * fade + jnp.dot(
                expo.astype(jnp.bfloat16), v, preferred_element_type=jnp.float32
            )

    def attend(s):
        attend_half(own_half(s), kv_own, s)
        wait_sibling(KV, s)
        attend_half(sib_half(s), kv_sib, s)

    def attend_step(s, carry):
        pass_on(KV, s)

        @pl.when(s > 0)
        def _():
            attend(s - 1)

        return carry

    lax.fori_loop(0, NZ, attend_step, 0)
    pass_on(W_OUT, 1)
    attend(NZ - 1)
    for h in range(HEADS_HERE):
        at = pl.ds(h * tokens, tokens)
        mixed_ref[:, h * HD : (h + 1) * HD] = (o_ref[at, :] / sum_ref[at, :]).astype(jnp.bfloat16)

    def rs_copy(s, d):
        u = (t + d) % NT
        return pltpu.make_async_remote_copy(
            src_ref=rs_send.at[s, u],
            dst_ref=rs_recv.at[s, d - 1],
            send_sem=rs_send_sem,
            recv_sem=rs_recv_sem.at[s],
            device_id=device(ctx, u),
        )

    def share(s):
        wait_sibling(W_OUT, s)
        for i, ref in enumerate((w_out_own, w_out_sib)):
            right = ref[s].reshape(half_c, ref.shape[-1])
            part = lax.dot_general(mixed_ref[...], right, NT_DIMS, preferred_element_type=jnp.float32)
            part = part.astype(jnp.bfloat16).reshape(NT, rows, half_c)
            rs_send[s, :, :, i * half_c : (i + 1) * half_c] = part
        for d in range(1, NT):
            rs_copy(s, d).start()

    def share_step(s, carry):
        @pl.when(s > 1)
        def _():
            pass_on(W_OUT, s)

        share(s - 1)
        return carry

    lax.fori_loop(1, NZ, share_step, 0)
    share(NZ - 1)

    def add_up(s, carry):
        whole = rs_recv.at[s]
        pltpu.make_async_copy(whole, whole, rs_recv_sem.at[s]).wait()
        total = rs_send[s, t].astype(jnp.float32)
        for d in range(1, NT):
            total += rs_recv[s, d - 1].astype(jnp.float32)
        total = total.astype(jnp.bfloat16)
        for i, half in enumerate((own_half(s), sib_half(s))):
            cols = pl.ds(pl.multiple_of(half * half_c, half_c), half_c)
            out_ref[:, cols] = total[:, i * half_c : (i + 1) * half_c]
        return carry

    lax.fori_loop(0, NZ, add_up, 0)

    finish_plane(W_IN, w_in_ref)
    finish_plane(W_OUT, w_out_ref)
    finish_plane(KV, kv_stage)
    for g in (W_IN, KV, W_OUT):
        finish_gather(g)
    for d in range(1, NT):
        norm_copy(d).wait_send()
    pltpu.make_async_copy(rs_recv, rs_recv, rs_send_sem).wait()


def per_device(NC, NT, NY, hidden_rows, norm_gain, w_qkv, w_out, doc_lengths, span_order):
    J = NY * CORES // 2
    NZ = NC // (NY * CORES)
    rows, D = hidden_rows.shape
    tokens = rows * NT
    k_rows, in_cols = w_qkv.shape
    out_rows, c_cols = w_out.shape
    qcols = HEADS_HERE * HD
    freq = THETA ** (-(np.arange(HD // 2, dtype=np.float64) * 2.0 / HD))
    freq = jnp.asarray(np.tile(freq, 2)[None, :].astype(np.float32))
    bf16, f32 = jnp.bfloat16, jnp.float32
    vmem = pl.BlockSpec(memory_space=pltpu.VMEM)
    smem = pl.BlockSpec(memory_space=pltpu.SMEM)
    anywhere = pl.BlockSpec(memory_space=pl.ANY)
    DMA = pltpu.SemaphoreType.DMA
    return pl.pallas_call(
        functools.partial(kernel, NZ, NY, NT),
        out_shape=jax.ShapeDtypeStruct((rows, D), bf16),
        in_specs=[smem, smem, vmem, vmem, vmem, anywhere, anywhere],
        out_specs=vmem,
        scratch_shapes=[
            pltpu.VMEM((NZ, J, k_rows, in_cols), bf16),
            pltpu.VMEM((NZ, J, k_rows, in_cols), bf16),
            pltpu.VMEM((NZ, J, tokens, 2 * HD), bf16),
            pltpu.VMEM((NZ, J, tokens, 2 * HD), bf16),
            pltpu.VMEM((NZ, J, c_cols, out_rows), bf16),
            pltpu.VMEM((NZ, J, c_cols, out_rows), bf16),
            pltpu.VMEM((NT, rows, D), bf16),
            pltpu.VMEM((tokens, in_cols), f32),
            pltpu.VMEM((HEADS_HERE * tokens, HD), bf16),
            pltpu.VMEM((tokens, 2 * HD), bf16),
            pltpu.VMEM((HEADS_HERE * tokens, HD), f32),
            pltpu.VMEM((HEADS_HERE * tokens, 1), f32),
            pltpu.VMEM((HEADS_HERE * tokens, 1), f32),
            pltpu.VMEM((tokens, qcols), bf16),
            pltpu.VMEM((NZ, NT, rows, 2 * J * c_cols), bf16),
            pltpu.VMEM((NZ, NT - 1, rows, 2 * J * c_cols), bf16),
            DMA((3, NZ, J)),
            DMA((3, NZ)),
            DMA((3, NY)),
            DMA((3,)),
            DMA((3,)),
            DMA((NT - 1,)),
            DMA((NT,)),
            DMA,
            DMA((NZ,)),
        ],
        compiler_params=pltpu.CompilerParams(
            collective_id=0, has_side_effects=True, vmem_limit_bytes=48 * 2**20
        ),
        cost_estimate=pl.CostEstimate(
            flops=2 * tokens * (D * in_cols + qcols * 2 * NC * tokens + out_rows * D),
            bytes_accessed=4 * rows * D,
            transcendentals=HEADS_HERE * tokens * tokens * NC,
        ),
    )(span_order, doc_lengths, hidden_rows, norm_gain, freq, w_qkv, w_out.T)


def build(mesh, NY):
    placed = (
        P(("context", "tensor"), None),
        P(),
        P("context", "tensor"),
        P("tensor", "context"),
        P(),
        P(),
    )
    return jax.shard_map(
        functools.partial(per_device, mesh.shape["context"], mesh.shape["tensor"], NY),
        mesh=mesh,
        in_specs=placed,
        out_specs=P(("context", "tensor"), None),
        check_vma=False,
    )


def solution(mesh):
    return build(mesh, Y_HI)
```

time: 461 us -> 151 us (0.33)
  waiting for transfers between devices: 398 us -> 0 us
  Pallas kernels: 0 us -> 145 us
  matrix products: 23.8 us -> 0 us
  other arithmetic: 14.4 us -> 0 us
  between operations: 13.6 us -> 0.02 us
    all_gather x5 -> x0, waiting for transfers between devices: 361 us -> none  [the longest x1 103 us: per_device(): lax.all_gather(w_qkv, 'context', axis=0, tiled=True)]
    pallas_call x0 -> x1, Pallas kernels: none -> 145 us  [per_device(): pl.pallas_call(functools.partial(kernel, NZ, NY, NT), out_shape=jax.Shape...]
    reduce_scatter x1 -> x0, waiting for transfers between devices: 35.6 us -> none  [per_device(): lax.psum_scatter(partial_sums.astype(jnp.bfloat16), 'tensor', scatter_dim...]
    dot_general x4 -> x0, matrix products: 23.8 us -> none  [the longest x1 9.98 us: per_device(): jnp.einsum('qhk,kd->qhd', expo.astype(jnp.bfloat16), value_block, preferr...]
    reduce_sum x6 -> x0, other arithmetic: 9.74 us -> none  [the longest x1 5.05 us: per_device(): total_new = jnp.sum(expo, axis=-1)]
  transfers between devices with their start and end apart: 6 -> 0, of which waited for: 6 -> 0; matrix products, arithmetic and copies ran while one was open for 6% -> 0% of each run, Pallas kernels for 0% -> 0%
where the time goes in v1:
time: 151 us; the launch traced here: 149 us
  Pallas kernels  145 us (96%)
  local copies, waits for them, and re-layouts  4.67 us (3%)
    pallas_call x1, Pallas kernels, per_device(): pl.pallas_call(functools.partial(kernel, NZ, NY, NT), out_shape=jax.Shape...  145 us
    unnamed x15, local copies, waits for them, and re-layouts  4.67 us

profile of v1, /device:TPU:1, one launch (start us, length us, event | category | flops | bytes accessed | tf_op | source)
XLA Modules:
  0.0 149.4 jit_solution(15812879223659226859)
XLA Ops:
  0.0 0.0 copy-start.6
  0.0 0.0 copy-start.4
  0.0 0.0 copy-start.5
  0.0 0.6 copy-done.6
  0.7 0.0 copy-done.4
  0.7 0.0 copy-done.5
  0.7 0.0 copy-start
  0.7 0.9 copy-done
  1.6 0.0 copy-start.1
  1.6 0.9 copy-done.1
  2.5 0.0 copy-start.2
  2.5 0.8 copy-done.2
  3.3 0.0 copy-start.3
  3.3 0.7 copy-done.3
  4.0 144.7 %shard_map.73 = bf16[16,4096]{1,0:T(8,128)(2,1)S(1)} custom-call(s32[128]{0:T(128)S(1)} %copy-done.4, s32[16]{0:T(128)S(1)} %copy-done.5, bf16[16,4096]{1,0:T(8,128)(2,1)S(1)} %copy-done, bf16[4096]{0:T(1024)(128)(2,1)S(1)} %copy-done.3, f32[1,128]{1,0:T(1,128)S(1)} %copy-done.6, bf16[64,768]{1,0:T(8,128)(2,1)S(1)} %copy-done.1, bf16[64,512]{1,0:T(8,128)(2,1)S(1)} %bitcast.1), custom_call_target="tpu_custom_call" | custom-call | flops 3489660928 | bytes 262144 | tf_op jit(solution)/shard_map/pallas_call | solution.py:365
  148.7 0.7 copy.9
Async XLA Ops:
  0.0 0.7 copy-start.6
  0.0 0.7 copy-start.4
  0.0 0.7 copy-start.5
  0.7 0.9 copy-start
  1.6 0.9 copy-start.1
  2.5 0.8 copy-start.2
  3.3 0.7 copy-start.3

commit v2 on v1

v2 whole, which is shorter than its diff:
```python
import functools
import math

import jax
import jax.numpy as jnp
import numpy as np
from jax import lax
from jax.experimental import pallas as pl
from jax.experimental.pallas import tpu as pltpu
from jax.sharding import PartitionSpec as P

HD = 128
HEADS_HERE = 4
SPAN = 64
THETA = 500000.0
Y_HI = 4
CORES = 2
MASKED = -1e30
NT_DIMS = (((1,), (1,)), ((), ()))

W_IN, KV, W_OUT = 0, 1, 2


def kernel(
    NZ,
    NY,
    NT,
    span_ref,
    len_ref,
    hidden_hbm,
    gain_hbm,
    freq_hbm,
    w_in_ref,
    w_out_ref,
    out_ref,
    hidden_ref,
    gain_ref,
    freq_ref,
    cos_ref,
    sin_ref,
    w_in_own,
    w_in_sib,
    kv_own,
    kv_sib,
    w_out_own,
    w_out_sib,
    normed_ref,
    acc_ref,
    q_ref,
    kv_stage,
    o_ref,
    top_ref,
    sum_ref,
    mixed_ref,
    rs_send,
    rs_recv,
    own_recv,
    sib_recv,
    plane_send,
    ring_send,
    sib_send,
    norm_send,
    norm_recv,
    rs_send_sem,
    rs_recv_sem,
    load_sem,
):
    PLANE = NY * CORES
    J = PLANE // 2
    rows, D = hidden_ref.shape
    tokens = rows * NT
    qcols = HEADS_HERE * HD
    piece_k = D // NZ
    half_cols = w_in_ref.shape[1] // 2
    half_c = J * w_out_ref.shape[0]
    order = ((0, 0), (1, 1), (3, 1), (2, 1)) if NY == 4 else ((0, 0), (1, 1))
    H = NZ // 2

    ctx = lax.axis_index("context")
    t = lax.axis_index("tensor")
    z = ctx // PLANE
    y = (ctx % PLANE) // CORES
    core = ctx % CORES
    my_class = y // (NY // 2)
    slot = (y % (NY // 2)) * CORES + core
    above = ((z + 1) % NZ) * PLANE + y * CORES + core
    below = ((z + NZ - 1) % NZ) * PLANE + y * CORES + core
    sibling = z * PLANE + y * CORES + (1 - core)

    def device(c, u):
        return {"context": c, "tensor": u}

    loads = [
        pltpu.make_async_copy(src, dst, load_sem.at[i])
        for i, (src, dst) in enumerate(
            ((hidden_hbm, hidden_ref), (gain_hbm, gain_ref), (freq_hbm, freq_ref))
        )
    ]
    for load in loads:
        load.start()

    own = (w_in_own, kv_own, w_out_own)
    sib = (w_in_sib, kv_sib, w_out_sib)

    barrier = pltpu.get_barrier_semaphore()
    for d in range(1, PLANE):
        c = z * PLANE + (ctx % PLANE + d) % PLANE
        pl.semaphore_signal(barrier, inc=1, device_id=device(c, t))
    for c in (above, below):
        pl.semaphore_signal(barrier, inc=1, device_id=device(c, t))
    for d in range(1, NT):
        pl.semaphore_signal(barrier, inc=1, device_id=device(ctx, (t + d) % NT))

    pl.semaphore_wait(barrier, PLANE - 1 + 2 + NT - 1)

    def plane_copies(g, src):
        copies = []
        if g == W_OUT:
            for d, _ in order:
                copies.append((d, my_class, src, own[g].at[0, slot], own_recv.at[g, 0, slot]))
        else:
            for d, _ in order:
                for c in range(CORES):
                    if g == W_IN:
                        half = src.at[:, c * half_cols : (c + 1) * half_cols]
                    else:
                        half = src.at[c * (tokens // 2) : (c + 1) * (tokens // 2), :]
                    n = half.shape[0]
                    part = pl.ds(pl.multiple_of(core * n, n), n)
                    copies.append((d, c, half, own[g].at[0, y, part], own_recv.at[g, 0, y]))
        for i, (d, c, half, dst, sem) in enumerate(copies):
            chip = z * PLANE + ((y + d) % NY) * CORES
            remote = functools.partial(
                pltpu.make_async_remote_copy,
                src_ref=half,
                dst_ref=dst,
                send_sem=plane_send.at[g, i],
                recv_sem=sem,
                device_id=device(chip + c, t),
            )
            local = functools.partial(pltpu.make_async_copy, half, dst, sem)
            yield d, c, remote, local

    def start_plane(g, src):
        for d, c, remote, local in plane_copies(g, src):
            if d == 0:
                pl.when(core == c)(lambda: local().start())
                pl.when(core != c)(lambda: remote().start())
            else:
                remote().start()

    def finish_plane(g, src):
        for d, c, remote, local in plane_copies(g, src):
            if d == 0:
                pl.when(core != c)(lambda: remote().wait_send())
            else:
                remote().wait_send()

    def take(g, q, j):
        unit = own[g].at[q, j]
        pltpu.make_async_copy(unit, unit, own_recv.at[g, q, j]).wait()
        pltpu.make_async_remote_copy(
            src_ref=unit,
            dst_ref=sib[g].at[q, j],
            send_sem=sib_send.at[g],
            recv_sem=sib_recv.at[g, q],
            device_id=device(sibling, t),
        ).start()

    def forward(g, q, j, to, q_there):
        pltpu.make_async_remote_copy(
            src_ref=own[g].at[q, j],
            dst_ref=own[g].at[q_there, j],
            send_sem=ring_send.at[g],
            recv_sem=own_recv.at[g, q_there, j],
            device_id=device(to, t),
        ).start()

    def pass_unit(g, s, j, from_below):
        up_last = H if from_below else H - 1
        down_last = H - 1 if from_below else H

        @pl.when(s == 0)
        def _():
            take(g, 0, j)
            if up_last > 0:
                forward(g, 0, j, above, 1)
            if down_last > 0:
                forward(g, 0, j, below, NZ - 1)

        @pl.when((s > 0) & (s < H))
        def _():
            take(g, s, j)
            pl.when(s < up_last)(lambda: forward(g, s, j, above, s + 1))
            take(g, NZ - s, j)
            pl.when(s < down_last)(lambda: forward(g, NZ - s, j, below, NZ - s - 1))

        @pl.when(s == H)
        def _():
            take(g, H, j)

    def pass_on(g, s):
        for j in range(J):
            pass_unit(g, s, j, j < J // 2)

    def pass_skewed(g, m):
        for i, (d, late) in enumerate(order):
            s = m - late

            @pl.when((s >= 0) & (s <= H))
            def _():
                pass_unit(g, s, (y + d) % NY, i < NY // 2)

    def for_slots(s, act):
        act(s)
        pl.when((s > 0) & (s < H))(lambda: act(NZ - s))

    def wait_sibling(g, q):
        whole = sib[g].at[q]
        pltpu.make_async_copy(whole, whole, sib_recv.at[g, q]).wait()

    def finish_gather(g):
        sent = own[g].at[pl.ds(0, NZ - 1)]
        pltpu.make_async_copy(sent, sent, ring_send.at[g]).wait()
        pltpu.make_async_copy(sib[g], sib[g], sib_send.at[g]).wait()

    def source_z(q):
        return (z + NZ - q) % NZ

    start_plane(W_IN, w_in_ref)

    for load in loads:
        load.wait()
    wide = hidden_ref[...].astype(jnp.float32)
    meansq = jnp.mean(wide * wide, axis=-1, keepdims=True)
    gain = gain_ref[...].astype(jnp.float32).reshape(1, D)
    normed_ref[t] = (wide * lax.rsqrt(meansq + 1e-5) * gain).astype(jnp.bfloat16)

    def norm_copy(d):
        return pltpu.make_async_remote_copy(
            src_ref=normed_ref.at[t],
            dst_ref=normed_ref.at[t],
            send_sem=norm_send.at[d - 1],
            recv_sem=norm_recv.at[t],
            device_id=device(ctx, (t + d) % NT),
        )

    for d in range(1, NT):
        norm_copy(d).start()

    start_plane(W_OUT, w_out_ref)

    row = lax.broadcasted_iota(jnp.int32, (tokens, 1), 0)
    source = jnp.zeros_like(row)
    for a in range(tokens // SPAN):
        source = jnp.where(row // SPAN == a, span_ref[ctx * (tokens // SPAN) + a], source)
    orig = source * SPAN + row % SPAN
    start = jnp.zeros_like(orig)
    end = jnp.int32(0)
    for i in range(len_ref.shape[0]):
        end = end + len_ref[i]
        start = jnp.where(end <= orig, jnp.maximum(start, end), start)

    angle = (orig - start).astype(jnp.float32) * freq_ref[...]
    lane = lax.broadcasted_iota(jnp.int32, (tokens, HD), 1)
    cos_ref[...] = jnp.cos(angle)
    sine = jnp.sin(angle)
    sin_ref[...] = jnp.where(lane < HD // 2, -sine, sine)

    acc_ref[...] = jnp.zeros_like(acc_ref)
    top_ref[...] = jnp.full_like(top_ref, MASKED)
    sum_ref[...] = jnp.zeros_like(sum_ref)
    o_ref[...] = jnp.zeros_like(o_ref)

    def project(q):
        wait_sibling(W_IN, q)
        cols = pl.ds(pl.multiple_of(source_z(q) * piece_k, piece_k), piece_k)
        left = normed_ref[:, :, cols].reshape(tokens, piece_k)
        for c, ref in ((core, w_in_own), (1 - core, w_in_sib)):
            right = ref[q].reshape(piece_k, half_cols)
            acc_ref[c] += jnp.dot(left, right, preferred_element_type=jnp.float32)

    def project_step(m, carry):
        pass_skewed(W_IN, m)

        @pl.when(m == H)
        def _():
            pass_on(W_OUT, 0)

        @pl.when(m == 2)
        def _():
            for d in range(1, NT):
                other = (t + NT - d) % NT
                block = normed_ref.at[other]
                pltpu.make_async_copy(block, block, norm_recv.at[other]).wait()

        @pl.when(m >= 2)
        def _():
            for_slots(m - 2, project)

        return carry

    lax.fori_loop(0, H + 2, project_step, 0)
    project(H)

    scale = math.log2(math.e) / HD**0.5
    cosine = cos_ref[...]
    sine = sin_ref[...]

    def rotate(x):
        return x * cosine + pltpu.roll(x, HD // 2, 1) * sine

    def columns(i):
        per = half_cols // HD
        return acc_ref[i // per, :, (i % per) * HD : (i % per + 1) * HD]

    kv_stage[:, :HD] = rotate(columns(HEADS_HERE)).astype(jnp.bfloat16)
    kv_stage[:, HD:] = columns(HEADS_HERE + 1).astype(jnp.bfloat16)
    start_plane(KV, kv_stage)
    for h in range(HEADS_HERE):
        q_ref[h * tokens : (h + 1) * tokens, :] = (rotate(columns(h)) * scale).astype(jnp.bfloat16)

    keys = J * tokens
    spans = keys // SPAN

    def attend_half(at, c, ref, q):
        lane = lax.broadcasted_iota(jnp.int32, (1, keys), 1)
        key_source = jnp.zeros_like(lane)
        for a in range(spans):
            held = span_ref[2 * (at * spans + a) + c]
            key_source = jnp.where(lane // SPAN == a, held, key_source)
        key_orig = key_source * SPAN + lane % SPAN
        allowed = (start <= key_orig) & (key_orig <= orig)
        cap = jnp.where(allowed, 3e38, MASKED)
        k = ref[q, :, :, :HD].reshape(keys, HD)
        v = ref[q, :, :, HD:].reshape(keys, HD)
        scores = lax.dot_general(q_ref[...], k, NT_DIMS, preferred_element_type=jnp.float32)
        weights = []
        for h in range(HEADS_HERE):
            rows_h = slice(h * tokens, (h + 1) * tokens)
            mine = jnp.minimum(scores[rows_h], cap)
            old = top_ref[rows_h, :]
            new = jnp.maximum(old, jnp.max(mine, axis=1, keepdims=True))
            fade = jnp.exp2(old - new)
            top_ref[rows_h, :] = new
            expo = [jnp.exp2(mine[:, i : i + HD] - new) for i in range(0, keys, HD)]
            sum_ref[rows_h, :] = sum_ref[rows_h, :] * fade + functools.reduce(jnp.add, expo)
            o_ref[rows_h, :] = o_ref[rows_h, :] * fade
            weights.append(jnp.concatenate([e.astype(jnp.bfloat16) for e in expo], axis=1))
        weights = jnp.concatenate(weights, axis=0)
        o_ref[...] += jnp.dot(weights, v, preferred_element_type=jnp.float32)

    def attend(q):
        attend_half(source_z(q), core, kv_own, q)
        wait_sibling(KV, q)
        attend_half(source_z(q), 1 - core, kv_sib, q)

    def attend_step(m, carry):
        pass_skewed(KV, m)

        @pl.when(m == 1)
        def _():
            pass_on(W_OUT, 1)

        @pl.when(m == H)
        def _():
            pass_on(W_OUT, min(2, H))

        @pl.when(m >= 2)
        def _():
            for_slots(m - 2, attend)

        return carry

    lax.fori_loop(0, H + 2, attend_step, 0)
    attend(H)
    for h in range(HEADS_HERE):
        at = pl.ds(h * tokens, tokens)
        mixed_ref[:, h * HD : (h + 1) * HD] = (
            o_ref[at, :] / jnp.sum(sum_ref[at, :], axis=1, keepdims=True)
        ).astype(jnp.bfloat16)

    def rs_copy(q, d):
        u = (t + d) % NT
        return pltpu.make_async_remote_copy(
            src_ref=rs_send.at[q, u],
            dst_ref=rs_recv.at[q, d - 1],
            send_sem=rs_send_sem,
            recv_sem=rs_recv_sem.at[q],
            device_id=device(ctx, u),
        )

    def share(q):
        wait_sibling(W_OUT, q)
        for i, ref in enumerate((w_out_own, w_out_sib)):
            right = ref[q].reshape(half_c, ref.shape[-1])
            part = lax.dot_general(mixed_ref[...], right, NT_DIMS, preferred_element_type=jnp.float32)
            part = part.astype(jnp.bfloat16).reshape(NT, rows, half_c)
            rs_send[q, :, :, i * half_c : (i + 1) * half_c] = part
        for d in range(1, NT):
            rs_copy(q, d).start()

    def add_up(q):
        whole = rs_recv.at[q]
        pltpu.make_async_copy(whole, whole, rs_recv_sem.at[q]).wait()
        total = rs_send[q, t].astype(jnp.float32)
        for d in range(1, NT):
            total += rs_recv[q, d - 1].astype(jnp.float32)
        total = total.astype(jnp.bfloat16)
        for i, c in enumerate((core, 1 - core)):
            cols = pl.ds(pl.multiple_of((source_z(q) * 2 + c) * half_c, half_c), half_c)
            out_ref[:, cols] = total[:, i * half_c : (i + 1) * half_c]

    def share_step(s, carry):
        @pl.when(s > 2)
        def _():
            pass_on(W_OUT, s)

        for_slots(s - 1, share)

        @pl.when(s > 2)
        def _():
            for_slots(s - 3, add_up)

        return carry

    lax.fori_loop(1, H + 1, share_step, 0)
    share(H)

    def add_step(s, carry):
        for_slots(s, add_up)
        return carry

    lax.fori_loop(max(H - 2, 0), H + 1, add_step, 0)

    finish_plane(W_IN, w_in_ref)
    finish_plane(W_OUT, w_out_ref)
    finish_plane(KV, kv_stage)
    for g in (W_IN, KV, W_OUT):
        finish_gather(g)
    for d in range(1, NT):
        norm_copy(d).wait_send()
    pltpu.make_async_copy(rs_recv, rs_recv, rs_send_sem).wait()


def per_device(NC, NT, NY, hidden_rows, norm_gain, w_qkv, w_out, doc_lengths, span_order):
    J = NY * CORES // 2
    NZ = NC // (NY * CORES)
    rows, D = hidden_rows.shape
    tokens = rows * NT
    k_rows, in_cols = w_qkv.shape
    out_rows, c_cols = w_out.shape
    qcols = HEADS_HERE * HD
    freq = THETA ** (-(np.arange(HD // 2, dtype=np.float64) * 2.0 / HD))
    freq = jnp.asarray(np.tile(freq, 2)[None, :].astype(np.float32))
    bf16, f32 = jnp.bfloat16, jnp.float32
    vmem = pl.BlockSpec(memory_space=pltpu.VMEM)
    smem = pl.BlockSpec(memory_space=pltpu.SMEM)
    hbm = pl.BlockSpec(memory_space=pltpu.HBM)
    DMA = pltpu.SemaphoreType.DMA
    return pl.pallas_call(
        functools.partial(kernel, NZ, NY, NT),
        out_shape=jax.ShapeDtypeStruct((rows, D), bf16),
        in_specs=[smem, smem, hbm, hbm, hbm, hbm, hbm],
        out_specs=vmem,
        scratch_shapes=[
            pltpu.VMEM((rows, D), bf16),
            pltpu.VMEM((D,), bf16),
            pltpu.VMEM((1, HD), f32),
            pltpu.VMEM((tokens, HD), f32),
            pltpu.VMEM((tokens, HD), f32),
            pltpu.VMEM((NZ, NY, CORES * k_rows, in_cols // 2), bf16),
            pltpu.VMEM((NZ, NY, CORES * k_rows, in_cols // 2), bf16),
            pltpu.VMEM((NZ, NY, tokens, 2 * HD), bf16),
            pltpu.VMEM((NZ, NY, tokens, 2 * HD), bf16),
            pltpu.VMEM((NZ, J, c_cols, out_rows), bf16),
            pltpu.VMEM((NZ, J, c_cols, out_rows), bf16),
            pltpu.VMEM((NT, rows, D), bf16),
            pltpu.VMEM((CORES, tokens, in_cols // 2), f32),
            pltpu.VMEM((HEADS_HERE * tokens, HD), bf16),
            pltpu.VMEM((tokens, 2 * HD), bf16),
            pltpu.VMEM((HEADS_HERE * tokens, HD), f32),
            pltpu.VMEM((HEADS_HERE * tokens, HD), f32),
            pltpu.VMEM((HEADS_HERE * tokens, HD), f32),
            pltpu.VMEM((tokens, qcols), bf16),
            pltpu.VMEM((NZ, NT, rows, 2 * J * c_cols), bf16),
            pltpu.VMEM((NZ, NT - 1, rows, 2 * J * c_cols), bf16),
            DMA((3, NZ, J)),
            DMA((3, NZ)),
            DMA((3, 2 * NY)),
            DMA((3,)),
            DMA((3,)),
            DMA((NT - 1,)),
            DMA((NT,)),
            DMA,
            DMA((NZ,)),
            DMA((3,)),
        ],
        compiler_params=pltpu.CompilerParams(
            collective_id=0, has_side_effects=True, vmem_limit_bytes=62 * 2**20
        ),
        cost_estimate=pl.CostEstimate(
            flops=2 * tokens * (D * in_cols + qcols * 2 * NC * tokens + out_rows * D),
            bytes_accessed=4 * rows * D,
            transcendentals=HEADS_HERE * tokens * tokens * NC,
        ),
    )(span_order, doc_lengths, hidden_rows, norm_gain, freq, w_qkv, w_out.T)


def build(mesh, NY):
    placed = (
        P(("context", "tensor"), None),
        P(),
        P("context", "tensor"),
        P("tensor", "context"),
        P(),
        P(),
    )
    return jax.shard_map(
        functools.partial(per_device, mesh.shape["context"], mesh.shape["tensor"], NY),
        mesh=mesh,
        in_specs=placed,
        out_specs=P(("context", "tensor"), None),
        check_vma=False,
    )


def solution(mesh):
    return build(mesh, Y_HI)
```

time: 151 us -> 113 us (0.75); the launches traced: 149 us -> 113 us
  Pallas kernels: 145 us -> 112 us
  local copies, waits for them, and re-layouts: 4.67 us -> 1.57 us
    pallas_call x1, Pallas kernels: 145 us -> 112 us  [per_device(): pl.pallas_call(functools.partial(kernel, NZ, NY, NT), out_shape=jax.Shape...]
    unnamed x15 -> x1, local copies, waits for them, and re-layouts: 4.67 us -> 1.57 us
where the time goes in v2:
time: 113 us
  Pallas kernels  112 us (99%)
  local copies, waits for them, and re-layouts  1.57 us (1%)
    pallas_call x1, Pallas kernels, per_device(): pl.pallas_call(functools.partial(kernel, NZ, NY, NT), out_shape=jax.Shape...  112 us

profile of v2, /device:TPU:1, one launch (start us, length us, event | category | flops | bytes accessed | tf_op | source)
XLA Modules:
  0.0 113.2 jit_solution(18209835515139375645)
XLA Ops:
  0.0 111.7 %shard_map.73 = bf16[16,4096]{1,0:T(8,128)(2,1)} custom-call(s32[128]{0:T(128)} %span_ref.1, s32[16]{0:T(128)} %len_ref.1, bf16[16,4096]{1,0:T(8,128)(2,1)} %hidden_hbm.1, bf16[4096]{0:T(1024)(128)(2,1)} %gain_hbm.1, f32[1,128]{1,0:T(1,128)} %constant.2.clone.freq_hbm, bf16[64,768]{1,0:T(8,128)(2,1)} %w_in_ref.1, bf16[64,512]{1,0:T(8,128)(2,1)} %bitcast.1), custom_call_target="tpu_custom_call" | custom-call | flops 3489660928 | bytes 262144 | tf_op jit(solution)/shard_map/pallas_call | solution.py:461
  111.7 1.6 %copy.9 = bf16[16,4096]{1,0:T(8,128)(2,1)} copy(bf16[16,4096]{1,0:T(8,128)(2,1)} %shard_map.73) | data formatting | bytes 262144

commit v3 on v2

--- a/solution.py
+++ b/solution.py
@@ -18,7 +18,8 @@
 MASKED = -1e30
 NT_DIMS = (((1,), (1,)), ((), ()))
 
-W_IN, KV, W_OUT = 0, 1, 2
+W_KV, W_Q, KV, W_OUT = 0, 1, 2, 3
+GATHERS = 4
 
 
 def kernel(
@@ -38,14 +39,17 @@
     freq_ref,
     cos_ref,
     sin_ref,
-    w_in_own,
-    w_in_sib,
+    w_kv_own,
+    w_kv_sib,
+    w_q_own,
+    w_q_sib,
     kv_own,
     kv_sib,
     w_out_own,
     w_out_sib,
     normed_ref,
-    acc_ref,
+    acc_kv,
+    acc_q,
     q_ref,
     kv_stage,
     o_ref,
@@ -71,9 +75,8 @@
     tokens = rows * NT
     qcols = HEADS_HERE * HD
     piece_k = D // NZ
-    half_cols = w_in_ref.shape[1] // 2
     half_c = J * w_out_ref.shape[0]
-    order = ((0, 0), (1, 1), (3, 1), (2, 1)) if NY == 4 else ((0, 0), (1, 1))
+    order = (0, 1, 3, 2) if NY == 4 else (0, 1)
     H = NZ // 2
 
     ctx = lax.axis_index("context")
@@ -99,8 +102,8 @@
     for load in loads:
         load.start()
 
-    own = (w_in_own, kv_own, w_out_own)
-    sib = (w_in_sib, kv_sib, w_out_sib)
+    own = (w_kv_own, w_q_own, kv_own, w_out_own)
+    sib = (w_kv_sib, w_q_sib, kv_sib, w_out_sib)
 
     barrier = pltpu.get_barrier_semaphore()
     for d in range(1, PLANE):
@@ -116,13 +119,15 @@
     def plane_copies(g, src):
         copies = []
         if g == W_OUT:
-            for d, _ in order:
+            for d in order:
                 copies.append((d, my_class, src, own[g].at[0, slot], own_recv.at[g, 0, slot]))
         else:
-            for d, _ in order:
+            for d in order:
                 for c in range(CORES):
-                    if g == W_IN:
-                        half = src.at[:, c * half_cols : (c + 1) * half_cols]
+                    if g == W_KV:
+                        half = src.at[:, qcols + c * HD : qcols + (c + 1) * HD]
+                    elif g == W_Q:
+                        half = src.at[:, c * qcols // 2 : (c + 1) * qcols // 2]
                     else:
                         half = src.at[c * (tokens // 2) : (c + 1) * (tokens // 2), :]
                     n = half.shape[0]
@@ -176,44 +181,53 @@
             device_id=device(to, t),
         ).start()
 
-    def pass_unit(g, s, j, from_below):
-        up_last = H if from_below else H - 1
-        down_last = H - 1 if from_below else H
-
-        @pl.when(s == 0)
-        def _():
+    def when(condition, act):
+        if isinstance(condition, bool):
+            if condition:
+                act()
+        else:
+            pl.when(condition)(act)
+
+    def pass_unit(g, s, i):
+        first = i < NY // 2
+        j = (y + (i + i // 2 * (1 - 2 * (i % 2)) if NY == 4 else i)) % NY
+        going_up = (s < H - 1) | ((s == H - 1) & first)
+        going_down = (s < H - 1) | ((s == H - 1) & (i >= NY // 2))
+
+        def nearest():
             take(g, 0, j)
-            if up_last > 0:
-                forward(g, 0, j, above, 1)
-            if down_last > 0:
-                forward(g, 0, j, below, NZ - 1)
-
-        @pl.when((s > 0) & (s < H))
-        def _():
+            when(going_up, lambda: forward(g, 0, j, above, 1))
+            when(going_down, lambda: forward(g, 0, j, below, NZ - 1))
+
+        def between():
             take(g, s, j)
-            pl.when(s < up_last)(lambda: forward(g, s, j, above, s + 1))
+            when(going_up, lambda: forward(g, s, j, above, s + 1))
             take(g, NZ - s, j)
-            pl.when(s < down_last)(lambda: forward(g, NZ - s, j, below, NZ - s - 1))
-
-        @pl.when(s == H)
-        def _():
-            take(g, H, j)
-
-    def pass_on(g, s):
-        for j in range(J):
-            pass_unit(g, s, j, j < J // 2)
-
-    def pass_skewed(g, m):
-        for i, (d, late) in enumerate(order):
-            s = m - late
-
-            @pl.when((s >= 0) & (s <= H))
-            def _():
-                pass_unit(g, s, (y + d) % NY, i < NY // 2)
+            when(going_down, lambda: forward(g, NZ - s, j, below, NZ - s - 1))
+
+        when(s == 0, nearest)
+        when((s > 0) & (s < H), between)
+        when(s == H, lambda: take(g, H, j))
+
+    def pass_on(g, s, lo=0, hi=NY):
+        def body(i, carry):
+            pass_unit(g, s, i)
+            return carry
+
+        if hi - lo == 1:
+            pass_unit(g, s, lo)
+        else:
+            lax.fori_loop(lo, hi, body, 0)
 
     def for_slots(s, act):
-        act(s)
-        pl.when((s > 0) & (s < H))(lambda: act(NZ - s))
+        def body(i, carry):
+            act(s + i * (NZ - 2 * s))
+            return carry
+
+        if isinstance(s, int):
+            lax.fori_loop(0, 2 if 0 < s < H else 1, body, 0)
+        else:
+            lax.fori_loop(0, 2 - (s // H) - (1 - (s + H - 1) // H), body, 0)
 
     def wait_sibling(g, q):
         whole = sib[g].at[q]
@@ -227,7 +241,10 @@
     def source_z(q):
         return (z + NZ - q) % NZ
 
-    start_plane(W_IN, w_in_ref)
+    start_plane(W_KV, w_in_ref)
+    start_plane(W_Q, w_in_ref)
+    pass_on(W_KV, 0, 0, 1)
+    pass_on(W_Q, 0, 0, 1)
 
     for load in loads:
         load.wait()
@@ -248,6 +265,8 @@
     for d in range(1, NT):
         norm_copy(d).start()
 
+    pass_on(W_KV, 1, 0, 1)
+    pass_on(W_KV, 0, 1)
     start_plane(W_OUT, w_out_ref)
 
     row = lax.broadcasted_iota(jnp.int32, (tokens, 1), 0)
@@ -267,58 +286,57 @@
     sine = jnp.sin(angle)
     sin_ref[...] = jnp.where(lane < HD // 2, -sine, sine)
 
-    acc_ref[...] = jnp.zeros_like(acc_ref)
+    acc_kv[...] = jnp.zeros_like(acc_kv)
+    acc_q[...] = jnp.zeros_like(acc_q)
     top_ref[...] = jnp.full_like(top_ref, MASKED)
     sum_ref[...] = jnp.zeros_like(sum_ref)
     o_ref[...] = jnp.zeros_like(o_ref)
 
-    def project(q):
-        wait_sibling(W_IN, q)
+    def project(g, acc, q):
+        wait_sibling(g, q)
         cols = pl.ds(pl.multiple_of(source_z(q) * piece_k, piece_k), piece_k)
         left = normed_ref[:, :, cols].reshape(tokens, piece_k)
-        for c, ref in ((core, w_in_own), (1 - core, w_in_sib)):
-            right = ref[q].reshape(piece_k, half_cols)
-            acc_ref[c] += jnp.dot(left, right, preferred_element_type=jnp.float32)
-
-    def project_step(m, carry):
-        pass_skewed(W_IN, m)
-
-        @pl.when(m == H)
-        def _():
-            pass_on(W_OUT, 0)
-
-        @pl.when(m == 2)
-        def _():
-            for d in range(1, NT):
-                other = (t + NT - d) % NT
-                block = normed_ref.at[other]
-                pltpu.make_async_copy(block, block, norm_recv.at[other]).wait()
-
-        @pl.when(m >= 2)
-        def _():
-            for_slots(m - 2, project)
-
-        return carry
-
-    lax.fori_loop(0, H + 2, project_step, 0)
-    project(H)
+        for c, ref in ((core, own[g]), (1 - core, sib[g])):
+            right = ref[q].reshape(piece_k, ref.shape[-1])
+            acc[c] += jnp.dot(left, right, preferred_element_type=jnp.float32)
+
+    project_kv = functools.partial(project, W_KV, acc_kv)
+    project_q = functools.partial(project, W_Q, acc_q)
 
     scale = math.log2(math.e) / HD**0.5
-    cosine = cos_ref[...]
-    sine = sin_ref[...]
 
     def rotate(x):
-        return x * cosine + pltpu.roll(x, HD // 2, 1) * sine
-
-    def columns(i):
-        per = half_cols // HD
-        return acc_ref[i // per, :, (i % per) * HD : (i % per + 1) * HD]
-
-    kv_stage[:, :HD] = rotate(columns(HEADS_HERE)).astype(jnp.bfloat16)
-    kv_stage[:, HD:] = columns(HEADS_HERE + 1).astype(jnp.bfloat16)
+        return x * cos_ref[...] + pltpu.roll(x, HD // 2, 1) * sin_ref[...]
+
+    for s in range(2, H + 1):
+        pass_on(W_KV, s, 0, 1)
+        pass_on(W_KV, s - 1, 1)
+        pass_on(W_Q, s - 2, 1 if s == 2 else 0)
+    for d in range(1, NT):
+        other = (t + NT - d) % NT
+        block = normed_ref.at[other]
+        pltpu.make_async_copy(block, block, norm_recv.at[other]).wait()
+    for s in range(H - 1):
+        for_slots(s, project_kv)
+    pass_on(W_KV, H, 1)
+    for s in range(H - 1, H + 1):
+        for_slots(s, project_kv)
+    kv_stage[:, :HD] = rotate(acc_kv[0]).astype(jnp.bfloat16)
+    kv_stage[:, HD:] = acc_kv[1].astype(jnp.bfloat16)
     start_plane(KV, kv_stage)
+
+    pass_on(W_Q, H - 1)
+    pass_on(W_OUT, 0)
+    for s in range(H - 2):
+        for_slots(s, project_q)
+    pass_on(KV, 0, 0, 1)
+    pass_on(W_Q, H)
+    for s in range(H - 2, H + 1):
+        for_slots(s, project_q)
     for h in range(HEADS_HERE):
-        q_ref[h * tokens : (h + 1) * tokens, :] = (rotate(columns(h)) * scale).astype(jnp.bfloat16)
+        per = HEADS_HERE // 2
+        x = acc_q[h // per, :, (h % per) * HD : (h % per + 1) * HD]
+        q_ref[h * tokens : (h + 1) * tokens, :] = (rotate(x) * scale).astype(jnp.bfloat16)
 
     keys = J * tokens
     spans = keys // SPAN
@@ -356,24 +374,15 @@
         attend_half(source_z(q), 1 - core, kv_sib, q)
 
     def attend_step(m, carry):
-        pass_skewed(KV, m)
-
-        @pl.when(m == 1)
-        def _():
-            pass_on(W_OUT, 1)
-
-        @pl.when(m == H)
-        def _():
-            pass_on(W_OUT, min(2, H))
-
-        @pl.when(m >= 2)
-        def _():
-            for_slots(m - 2, attend)
-
+        pl.when(m <= H)(lambda: pass_on(KV, m, 0, 1))
+        pl.when(m <= H + 1)(lambda: pass_on(KV, m - 1, 1))
+        pl.when(m == min(2, H))(lambda: pass_on(W_OUT, 1))
+        if H > 2:
+            pl.when(m == H)(lambda: pass_on(W_OUT, 2))
+        pl.when(m >= 2)(lambda: for_slots(m - 2, attend))
         return carry
 
-    lax.fori_loop(0, H + 2, attend_step, 0)
-    attend(H)
+    lax.fori_loop(1, H + 3, attend_step, 0)
     for h in range(HEADS_HERE):
         at = pl.ds(h * tokens, tokens)
         mixed_ref[:, h * HD : (h + 1) * HD] = (
@@ -412,10 +421,7 @@
             out_ref[:, cols] = total[:, i * half_c : (i + 1) * half_c]
 
     def share_step(s, carry):
-        @pl.when(s > 2)
-        def _():
-            pass_on(W_OUT, s)
-
+        pl.when(s > min(2, H - 1))(lambda: pass_on(W_OUT, s))
         for_slots(s - 1, share)
 
         @pl.when(s > 2)
@@ -433,10 +439,11 @@
 
     lax.fori_loop(max(H - 2, 0), H + 1, add_step, 0)
 
-    finish_plane(W_IN, w_in_ref)
+    finish_plane(W_KV, w_in_ref)
+    finish_plane(W_Q, w_in_ref)
     finish_plane(W_OUT, w_out_ref)
     finish_plane(KV, kv_stage)
-    for g in (W_IN, KV, W_OUT):
+    for g in range(GATHERS):
         finish_gather(g)
     for d in range(1, NT):
         norm_copy(d).wait_send()
@@ -469,14 +476,17 @@
             pltpu.VMEM((1, HD), f32),
             pltpu.VMEM((tokens, HD), f32),
             pltpu.VMEM((tokens, HD), f32),
-            pltpu.VMEM((NZ, NY, CORES * k_rows, in_cols // 2), bf16),
-            pltpu.VMEM((NZ, NY, CORES * k_rows, in_cols // 2), bf16),
+            pltpu.VMEM((NZ, NY, CORES * k_rows, HD), bf16),
+            pltpu.VMEM((NZ, NY, CORES * k_rows, HD), bf16),
+            pltpu.VMEM((NZ, NY, CORES * k_rows, qcols // 2), bf16),
+            pltpu.VMEM((NZ, NY, CORES * k_rows, qcols // 2), bf16),
             pltpu.VMEM((NZ, NY, tokens, 2 * HD), bf16),
             pltpu.VMEM((NZ, NY, tokens, 2 * HD), bf16),
             pltpu.VMEM((NZ, J, c_cols, out_rows), bf16),
             pltpu.VMEM((NZ, J, c_cols, out_rows), bf16),
             pltpu.VMEM((NT, rows, D), bf16),
-            pltpu.VMEM((CORES, tokens, in_cols // 2), f32),
+            pltpu.VMEM((CORES, tokens, HD), f32),
+            pltpu.VMEM((CORES, tokens, qcols // 2), f32),
             pltpu.VMEM((HEADS_HERE * tokens, HD), bf16),
             pltpu.VMEM((tokens, 2 * HD), bf16),
             pltpu.VMEM((HEADS_HERE * tokens, HD), f32),
@@ -485,11 +495,11 @@
             pltpu.VMEM((tokens, qcols), bf16),
             pltpu.VMEM((NZ, NT, rows, 2 * J * c_cols), bf16),
             pltpu.VMEM((NZ, NT - 1, rows, 2 * J * c_cols), bf16),
-            DMA((3, NZ, J)),
-            DMA((3, NZ)),
-            DMA((3, 2 * NY)),
-            DMA((3,)),
-            DMA((3,)),
+            DMA((GATHERS, NZ, J)),
+            DMA((GATHERS, NZ)),
+            DMA((GATHERS, 2 * NY)),
+            DMA((GATHERS,)),
+            DMA((GATHERS,)),
             DMA((NT - 1,)),
             DMA((NT,)),
             DMA,

time: 113 us -> 108 us (0.956)
  Pallas kernels: 112 us -> 106 us
    pallas_call x1, Pallas kernels: 112 us -> 106 us  [per_device(): pl.pallas_call(functools.partial(kernel, NZ, NY, NT), out_shape=jax.Shape...]
where the time goes in v3:
time: 108 us
  Pallas kernels  106 us (98%)
  local copies, waits for them, and re-layouts  1.57 us (1%)
    pallas_call x1, Pallas kernels, per_device(): pl.pallas_call(functools.partial(kernel, NZ, NY, NT), out_shape=jax.Shape...  106 us

profile of v3, /device:TPU:1, one launch (start us, length us, event | category | flops | bytes accessed | tf_op | source)
XLA Modules:
  0.0 107.5 jit_solution(14566407327247103173)
XLA Ops:
  0.0 106.0 %shard_map.73 = bf16[16,4096]{1,0:T(8,128)(2,1)} custom-call(s32[128]{0:T(128)} %span_ref.1, s32[16]{0:T(128)} %len_ref.1, bf16[16,4096]{1,0:T(8,128)(2,1)} %hidden_hbm.1, bf16[4096]{0:T(1024)(128)(2,1)} %gain_hbm.1, f32[1,128]{1,0:T(1,128)} %constant.2.clone.freq_hbm, bf16[64,768]{1,0:T(8,128)(2,1)} %w_in_ref.1, bf16[64,512]{1,0:T(8,128)(2,1)} %bitcast.1), custom_call_target="tpu_custom_call" | custom-call | flops 3489660928 | bytes 262144 | tf_op jit(solution)/shard_map/pallas_call | solution.py:468
  106.0 1.6 %copy.9 = bf16[16,4096]{1,0:T(8,128)(2,1)} copy(bf16[16,4096]{1,0:T(8,128)(2,1)} %shard_map.73) | data formatting | bytes 262144

commit v4 on v3

--- a/solution.py
+++ b/solution.py
@@ -20,6 +20,8 @@
 
 W_KV, W_Q, KV, W_OUT = 0, 1, 2, 3
 GATHERS = 4
+Z_OUT = 0
+Z_GATHERS = 1
 
 
 def kernel(
@@ -47,6 +49,7 @@
     kv_sib,
     w_out_own,
     w_out_sib,
+    z_out,
     normed_ref,
     acc_kv,
     acc_q,
@@ -68,6 +71,13 @@
     rs_send_sem,
     rs_recv_sem,
     load_sem,
+    z_recv,
+    y_recv,
+    z_sib_recv,
+    z_send,
+    y_send,
+    far_send,
+    z_sib_send,
 ):
     PLANE = NY * CORES
     J = PLANE // 2
@@ -241,6 +251,112 @@
     def source_z(q):
         return (z + NZ - q) % NZ
 
+    held = (z_out,)
+    near = (1, NY - 1) if NY > 2 else (1,)
+
+    def z_local(g, src):
+        return pltpu.make_async_copy(src, held[g].at[0, y, core], z_recv.at[g, 0])
+
+    def z_copy(g, src_place, dst_place, send_sem, recv_sem, to):
+        pltpu.make_async_remote_copy(
+            src_ref=held[g].at[src_place],
+            dst_ref=held[g].at[dst_place],
+            send_sem=send_sem.at[g],
+            recv_sem=recv_sem,
+            device_id=device(to, t),
+        ).start()
+
+    def z_wait(g, place, sem):
+        ref = held[g].at[place]
+        pltpu.make_async_copy(ref, ref, sem).wait()
+
+    def z_hand(g, q, row):
+        z_copy(g, (q, row, core), (q, row, core), z_sib_send, z_sib_recv.at[g, q], sibling)
+
+    def z_pass(g, s):
+        going_up = (s < H - 1) | ((s == H - 1) & (core == 0))
+        going_down = (s < H - 1) | ((s == H - 1) & (core == 1))
+
+        def up(q):
+            z_copy(g, (q, y, core), (q + 1, y, core), z_send, z_recv.at[g, q + 1], above)
+
+        def down(q):
+            there = (q + NZ - 1) % NZ
+            z_copy(g, (q, y, core), (there, y, core), z_send, z_recv.at[g, there], below)
+
+        def nearest():
+            z_wait(g, (0, y, core), z_recv.at[g, 0])
+            when(going_up, lambda: up(0))
+            when(going_down, lambda: down(0))
+            z_hand(g, 0, y)
+
+        def between():
+            z_wait(g, (s, y, core), z_recv.at[g, s])
+            when(going_up, lambda: up(s))
+            z_wait(g, (NZ - s, y, core), z_recv.at[g, NZ - s])
+            when(going_down, lambda: down(NZ - s))
+            z_hand(g, s, y)
+            z_hand(g, NZ - s, y)
+
+        def farthest():
+            z_wait(g, (H, y, core), z_recv.at[g, H])
+            z_hand(g, H, y)
+
+        when(s == 0, nearest)
+        when((s > 0) & (s < H), between)
+        when(s == H, farthest)
+
+    def chip_along_y(d):
+        return z * PLANE + ((y + d) % NY) * CORES + core
+
+    def y_push(g, q):
+        for d in near:
+            z_copy(g, (q, y, core), (q, y, core), y_send, y_recv.at[g, q, y], chip_along_y(d))
+
+    def y_take(g, q):
+        for d in near:
+            row = (y + d) % NY
+            z_wait(g, (q, row, core), y_recv.at[g, q, row])
+            if NY > 2:
+
+                @pl.when(q % 2 == (0 if d == 1 else 1))
+                def _():
+                    z_copy(g, (q, row, core), (q, row, core), far_send, y_recv.at[g, q, row], chip_along_y(NY - d))
+
+            z_hand(g, q, row)
+
+    def far_take(g, q):
+        if NY > 2:
+            row = (y + 2) % NY
+            z_wait(g, (q, row, core), y_recv.at[g, q, row])
+            z_hand(g, q, row)
+
+    def z_wait_sibling(g, q):
+        z_wait(g, (q, slice(None), 1 - core), z_sib_recv.at[g, q])
+
+    def z_finish(g):
+        for place, sem in (
+            ((pl.ds(0, NZ - 1), 0, 0), z_send),
+            ((slice(None), 0) if NY > 2 else (slice(None), 0, 0), y_send),
+            ((slice(None), slice(None), 0), z_sib_send),
+        ):
+            z_wait(g, place, sem.at[g])
+        if NY > 2:
+            z_wait(g, (slice(None), 0, 0), far_send.at[g])
+
+    def y_pushes(g, s):
+        for_slots(s, functools.partial(y_push, g))
+
+    def y_takes(g, s):
+        for_slots(s, functools.partial(y_take, g))
+
+    def far_takes(g, s):
+        for_slots(s, functools.partial(far_take, g))
+
+    w_out_first = w_out_ref.at[:, : qcols // 2]
+    w_out_rest = w_out_ref.at[:, qcols // 2 : qcols]
+    z_local(Z_OUT, w_out_rest).start()
+
     start_plane(W_KV, w_in_ref)
     start_plane(W_Q, w_in_ref)
     pass_on(W_KV, 0, 0, 1)
@@ -267,7 +383,8 @@
 
     pass_on(W_KV, 1, 0, 1)
     pass_on(W_KV, 0, 1)
-    start_plane(W_OUT, w_out_ref)
+    z_pass(Z_OUT, 0)
+    pass_on(W_Q, 1, 0, 1)
 
     row = lax.broadcasted_iota(jnp.int32, (tokens, 1), 0)
     source = jnp.zeros_like(row)
@@ -311,7 +428,15 @@
     for s in range(2, H + 1):
         pass_on(W_KV, s, 0, 1)
         pass_on(W_KV, s - 1, 1)
-        pass_on(W_Q, s - 2, 1 if s == 2 else 0)
+        pass_on(W_Q, s, 0, 1)
+        pass_on(W_Q, s - 2, 1)
+        if s == 2:
+            start_plane(W_OUT, w_out_first)
+        z_pass(Z_OUT, s - 1)
+        if s < 4:
+            y_pushes(Z_OUT, s - 2)
+    y_takes(Z_OUT, 0)
+    pass_on(W_OUT, 0)
     for d in range(1, NT):
         other = (t + NT - d) % NT
         block = normed_ref.at[other]
@@ -325,12 +450,16 @@
     kv_stage[:, HD:] = acc_kv[1].astype(jnp.bfloat16)
     start_plane(KV, kv_stage)
 
-    pass_on(W_Q, H - 1)
-    pass_on(W_OUT, 0)
+    pass_on(W_Q, H - 1, 1)
+    z_pass(Z_OUT, H)
     for s in range(H - 2):
         for_slots(s, project_q)
-    pass_on(KV, 0, 0, 1)
-    pass_on(W_Q, H)
+    pass_on(KV, 0)
+    y_pushes(Z_OUT, 2)
+    pass_on(KV, 1, 0, 1)
+    pass_on(W_Q, H, 1)
+    far_takes(Z_OUT, 0)
+    y_takes(Z_OUT, 1)
     for s in range(H - 2, H + 1):
         for_slots(s, project_q)
     for h in range(HEADS_HERE):
@@ -377,12 +506,16 @@
         pl.when(m <= H)(lambda: pass_on(KV, m, 0, 1))
         pl.when(m <= H + 1)(lambda: pass_on(KV, m - 1, 1))
         pl.when(m == min(2, H))(lambda: pass_on(W_OUT, 1))
-        if H > 2:
-            pl.when(m == H)(lambda: pass_on(W_OUT, 2))
-        pl.when(m >= 2)(lambda: for_slots(m - 2, attend))
+        if H == 4:
+            pl.when(m == H - 1)(lambda: pass_on(W_OUT, 2))
+            pl.when(m == H + 1)(lambda: pass_on(W_OUT, 3))
+        pl.when(m < H)(lambda: y_pushes(Z_OUT, m + 1))
+        pl.when((m >= 3) & (m <= H + 1))(lambda: y_takes(Z_OUT, m - 1))
+        pl.when(m >= 3)(lambda: far_takes(Z_OUT, m - 2))
+        for_slots(m - 2, attend)
         return carry
 
-    lax.fori_loop(1, H + 3, attend_step, 0)
+    lax.fori_loop(2, H + 3, attend_step, 0)
     for h in range(HEADS_HERE):
         at = pl.ds(h * tokens, tokens)
         mixed_ref[:, h * HD : (h + 1) * HD] = (
@@ -401,9 +534,13 @@
 
     def share(q):
         wait_sibling(W_OUT, q)
-        for i, ref in enumerate((w_out_own, w_out_sib)):
-            right = ref[q].reshape(half_c, ref.shape[-1])
-            part = lax.dot_general(mixed_ref[...], right, NT_DIMS, preferred_element_type=jnp.float32)
+        z_wait_sibling(Z_OUT, q)
+        for i, (c, ref) in enumerate(((core, w_out_own), (1 - core, w_out_sib))):
+            n = qcols // 2
+            right = ref[q].reshape(half_c, n)
+            part = lax.dot_general(mixed_ref[:, :n], right, NT_DIMS, preferred_element_type=jnp.float32)
+            right = z_out[q, pl.ds(c * (NY // 2), NY // 2)].reshape(half_c, n)
+            part += lax.dot_general(mixed_ref[:, n:], right, NT_DIMS, preferred_element_type=jnp.float32)
             part = part.astype(jnp.bfloat16).reshape(NT, rows, half_c)
             rs_send[q, :, :, i * half_c : (i + 1) * half_c] = part
         for d in range(1, NT):
@@ -421,7 +558,7 @@
             out_ref[:, cols] = total[:, i * half_c : (i + 1) * half_c]
 
     def share_step(s, carry):
-        pl.when(s > min(2, H - 1))(lambda: pass_on(W_OUT, s))
+        pl.when(s > (3 if H == 4 else 1))(lambda: pass_on(W_OUT, s))
         for_slots(s - 1, share)
 
         @pl.when(s > 2)
@@ -441,10 +578,12 @@
 
     finish_plane(W_KV, w_in_ref)
     finish_plane(W_Q, w_in_ref)
-    finish_plane(W_OUT, w_out_ref)
+    finish_plane(W_OUT, w_out_first)
     finish_plane(KV, kv_stage)
     for g in range(GATHERS):
         finish_gather(g)
+    for g in range(Z_GATHERS):
+        z_finish(g)
     for d in range(1, NT):
         norm_copy(d).wait_send()
     pltpu.make_async_copy(rs_recv, rs_recv, rs_send_sem).wait()
@@ -482,8 +621,9 @@
             pltpu.VMEM((NZ, NY, CORES * k_rows, qcols // 2), bf16),
             pltpu.VMEM((NZ, NY, tokens, 2 * HD), bf16),
             pltpu.VMEM((NZ, NY, tokens, 2 * HD), bf16),
-            pltpu.VMEM((NZ, J, c_cols, out_rows), bf16),
-            pltpu.VMEM((NZ, J, c_cols, out_rows), bf16),
+            pltpu.VMEM((NZ, J, c_cols, out_rows // 2), bf16),
+            pltpu.VMEM((NZ, J, c_cols, out_rows // 2), bf16),
+            pltpu.VMEM((NZ, NY, CORES, c_cols, out_rows // 2), bf16),
             pltpu.VMEM((NT, rows, D), bf16),
             pltpu.VMEM((CORES, tokens, HD), f32),
             pltpu.VMEM((CORES, tokens, qcols // 2), f32),
@@ -505,6 +645,13 @@
             DMA,
             DMA((NZ,)),
             DMA((3,)),
+            DMA((Z_GATHERS, NZ)),
+            DMA((Z_GATHERS, NZ, NY)),
+            DMA((Z_GATHERS, NZ)),
+            DMA((Z_GATHERS,)),
+            DMA((Z_GATHERS,)),
+            DMA((Z_GATHERS,)),
+            DMA((Z_GATHERS,)),
         ],
         compiler_params=pltpu.CompilerParams(
             collective_id=0, has_side_effects=True, vmem_limit_bytes=62 * 2**20

time: 108 us -> 107 us (level)
    pallas_call x1, Pallas kernels: 106 us -> 105 us  [per_device(): pl.pallas_call(functools.partial(kernel, NZ, NY, NT), out_shape=jax.Shape...]
where the time goes in v4:
time: 107 us; the launch traced here: 106 us
  Pallas kernels  105 us (98%)
  local copies, waits for them, and re-layouts  1.57 us (1%)
    pallas_call x1, Pallas kernels, per_device(): pl.pallas_call(functools.partial(kernel, NZ, NY, NT), out_shape=jax.Shape...  105 us

profile of v4, /device:TPU:1, one launch (start us, length us, event | category | flops | bytes accessed | tf_op | source)
XLA Modules:
  0.0 106.2 jit_solution(3218499115323106069)
XLA Ops:
  0.0 104.7 %shard_map.73 = bf16[16,4096]{1,0:T(8,128)(2,1)} custom-call(s32[128]{0:T(128)} %span_ref.1, s32[16]{0:T(128)} %len_ref.1, bf16[16,4096]{1,0:T(8,128)(2,1)} %hidden_hbm.1, bf16[4096]{0:T(1024)(128)(2,1)} %gain_hbm.1, f32[1,128]{1,0:T(1,128)} %constant.2.clone.freq_hbm, bf16[64,768]{1,0:T(8,128)(2,1)} %w_in_ref.1, bf16[64,512]{1,0:T(8,128)(2,1)} %bitcast.1), custom_call_target="tpu_custom_call" | custom-call | flops 3489660928 | bytes 262144 | tf_op jit(solution)/shard_map/pallas_call | solution.py:607
  104.7 1.6 %copy.9 = bf16[16,4096]{1,0:T(8,128)(2,1)} copy(bf16[16,4096]{1,0:T(8,128)(2,1)} %shard_map.73) | data formatting | bytes 262144

commit v5 on v4

--- a/solution.py
+++ b/solution.py
@@ -511,8 +511,8 @@
             pl.when(m == H + 1)(lambda: pass_on(W_OUT, 3))
         pl.when(m < H)(lambda: y_pushes(Z_OUT, m + 1))
         pl.when((m >= 3) & (m <= H + 1))(lambda: y_takes(Z_OUT, m - 1))
+        for_slots(m - 2, attend)
         pl.when(m >= 3)(lambda: far_takes(Z_OUT, m - 2))
-        for_slots(m - 2, attend)
         return carry
 
     lax.fori_loop(2, H + 3, attend_step, 0)
@@ -558,7 +558,7 @@
             out_ref[:, cols] = total[:, i * half_c : (i + 1) * half_c]
 
     def share_step(s, carry):
-        pl.when(s > (3 if H == 4 else 1))(lambda: pass_on(W_OUT, s))
+        pl.when(s == 2)(lambda: pass_on(W_OUT, H))
         for_slots(s - 1, share)
 
         @pl.when(s > 2)

time: 107 us -> 106 us (level)
  no operation moved by 1% of the time
where the time goes in v5:
time: 106 us; the launch traced here: 105 us
  Pallas kernels  104 us (98%)
  local copies, waits for them, and re-layouts  1.57 us (1%)
    pallas_call x1, Pallas kernels, per_device(): pl.pallas_call(functools.partial(kernel, NZ, NY, NT), out_shape=jax.Shape...  104 us

profile of v5, /device:TPU:1, one launch (start us, length us, event | category | flops | bytes accessed | tf_op | source)
XLA Modules:
  0.0 105.5 jit_solution(8190968514999029443)
XLA Ops:
  0.0 103.9 %shard_map.73 = bf16[16,4096]{1,0:T(8,128)(2,1)} custom-call(s32[128]{0:T(128)} %span_ref.1, s32[16]{0:T(128)} %len_ref.1, bf16[16,4096]{1,0:T(8,128)(2,1)} %hidden_hbm.1, bf16[4096]{0:T(1024)(128)(2,1)} %gain_hbm.1, f32[1,128]{1,0:T(1,128)} %constant.2.clone.freq_hbm, bf16[64,768]{1,0:T(8,128)(2,1)} %w_in_ref.1, bf16[64,512]{1,0:T(8,128)(2,1)} %bitcast.1), custom_call_target="tpu_custom_call" | custom-call | flops 3489660928 | bytes 262144 | tf_op jit(solution)/shard_map/pallas_call | solution.py:607
  103.9 1.6 %copy.9 = bf16[16,4096]{1,0:T(8,128)(2,1)} copy(bf16[16,4096]{1,0:T(8,128)(2,1)} %shard_map.73) | data formatting | bytes 262144
